TPU v7x, 32 devices: a whole 2x2x4 slice. The times are simulated.
32 devices in a mesh: lo: 4 (over y, x), hi: 8 (over z, core).
Axes of the slice: x: 2, y: 2, z: 4, core: 2. Of those that a mesh axis runs over, the one named last changes fastest.
Arguments:
- coefficients: float32 [2, 32, 8, 32768], P(None, None, None, ('lo', 'hi')), may hold values from -6 to 6
- angle_in: float32 [5, 64, 32768], P(None, None, ('lo', 'hi')), may hold values from -3.140625 to 3.140625
- angle_out: float32 [5, 32, 32768], P(None, None, ('lo', 'hi')), may hold values from -3.140625 to 3.140625
- interp: float32 [5, 32, 64], replicated, may hold values from -0.75 to 0.75
- destination: int32 [32, 1024], P(('lo', 'hi')), may hold values from 0 to 1023, each once within a row
Outputs:
- relaid: float32 [2, 32, 8, 32768], P(None, None, None, ('lo', 'hi'))
All inputs are finite; a program needn't handle non-finite values.
Results may differ from a plain program's by a relative error of at most 0.0001.
Values sent between devices are 32-bit elements; how exact they have to be, the bound alone decides.
A program may use at most 128 MiB of HBM per device.

v0:
```python
import jax
import jax.numpy as jnp
from jax import lax
from jax.sharding import PartitionSpec as P


def from_partner(x, axis, distance):
    return lax.ppermute(x, axis, [(i, i ^ 1 << distance) for i in range(lax.axis_size(axis))])


def widen(part):
    rows = part.shape[0]
    count = part.shape[1]
    half = part.shape[2]
    return jnp.broadcast_to(part[:, :, :, None], (rows, count, half, 2)).reshape(
        rows, count, 2 * half
    )


def apply_cols(matrix, real, imag, angle):
    rows = real.shape[0]
    count = real.shape[1]
    width = 2 * real.shape[2]
    cosine = jnp.cos(angle)[:, None, :]
    sine = jnp.sin(angle)[:, None, :]
    wide_re = widen(real)
    wide_im = widen(imag)
    yre = (wide_re * cosine - wide_im * sine).reshape(rows, count * width)
    yim = (wide_re * sine + wide_im * cosine).reshape(rows, count * width)
    outrows = matrix.shape[0]
    pre = jnp.dot(matrix, yre, precision=lax.Precision.HIGHEST, preferred_element_type=jnp.float32)
    pim = jnp.dot(matrix, yim, precision=lax.Precision.HIGHEST, preferred_element_type=jnp.float32)
    return (pre.reshape(outrows, count, width), pim.reshape(outrows, count, width))


def level(state, angle_in, angle_out, interp, axis, bit):
    width = state.shape[3]
    half = width // 2
    rank = state.shape[1]
    if axis == "lo":
        side = lax.axis_index("lo") // 2**bit % 2
    else:
        side = lax.axis_index("hi") // 2**bit % 2
    kept = lax.dynamic_slice_in_dim(state, side * half, half, 3)
    sent = lax.dynamic_slice_in_dim(state, (1 - side) * half, half, 3)
    if axis == "lo":
        got = from_partner(sent, "lo", bit)
    else:
        got = from_partner(sent, "hi", bit)
    shift_by = side * rank
    matrix = jnp.roll(interp, shift_by, axis=1)
    phases = jnp.roll(angle_in, shift_by, axis=0)
    real = jnp.concatenate([kept[0], got[0]], axis=0)
    imag = jnp.concatenate([kept[1], got[1]], axis=0)
    mre, mim = apply_cols(matrix, real, imag, phases)
    cosine = jnp.cos(angle_out)[:, None, :]
    sine = jnp.sin(angle_out)[:, None, :]
    zre = mre * cosine - mim * sine
    zim = mre * sine + mim * cosine
    return jnp.stack([zre, zim])


def shards(coefficients, angle_in, angle_out, interp, destination):
    state = coefficients
    lo_bits = lax.axis_size("lo").bit_length() - 1
    hi_bits = lax.axis_size("hi").bit_length() - 1
    step = 0
    for bit in range(lo_bits):
        state = level(state, angle_in[step], angle_out[step], interp[step], "lo", bit)
        step = step + 1
    for bit in range(hi_bits):
        state = level(state, angle_in[step], angle_out[step], interp[step], "hi", bit)
        step = step + 1
    taken = jnp.take(state, destination[0], axis=3)
    relaid = lax.all_to_all(taken, ("lo", "hi"), split_axis=3, concat_axis=3, tiled=True)
    return relaid


def solution(mesh):
    placed = (
        P(None, None, None, ("lo", "hi")),
        P(None, None, ("lo", "hi")),
        P(None, None, ("lo", "hi")),
        P(),
        P(("lo", "hi"), None),
    )
    return jax.shard_map(
        shards,
        mesh=mesh,
        in_specs=placed,
        out_specs=P(None, None, None, ("lo", "hi")),
        check_vma=False,
    )
```

profile of v0, /device:TPU:0, one launch (start us, length us, event | category | flops | bytes accessed | tf_op | source)
XLA Modules:
  0.0 345.0 jit_solution(7410564624529743322)
XLA Ops:
  0.0 1.4 constant_dynamic-slice_fusion
  1.5 3.0 collective-permute-start
  4.5 2.2 slice_bitcast_fusion.18
  6.6 3.4 fusion.23
  10.1 2.0 copy.16
  12.0 1.9 copy.18
  14.7 4.3 %cosine_bitcast_fusion = (f32[32,1024]{1,0:T(8,128)S(1)}, f32[32,1024]{1,0:T(8,128)}, f32[32,1024]{1,0:T(8,128)}, f32[32,1024]{1,0:T(8,128)}, f32[32,1024]{1,0:T...) fusion(f32[5,32,1024]{2,1,0:T(8,128)} %param.11), kind=kLoop, calls=%fused_computation.118 | loop fusion | bytes 1966080 | tf_op jit(solution)/shard_map/cos | solution.py:56
  19.0 8.7 %collective-permute-done = f32[2,32,8,512]{3,2,1,0:T(8,128)} collective-permute-done((f32[2,32,8,512]{3,2,1,0:T(8,128)S(1)}, f32[2,32,8,512]{3,2,1,0:T(8,128)}, u32[]{:S(2)}, u32[]{:S(2)}) %collective-permute-start) | collective-permute-done | bytes 1048608 | tf_op jit(solution)/shard_map/ppermute | solution.py:8
  30.1 1.8 copy.15
  32.0 2.1 copy.17
  35.5 3.1 broadcast_in_dim.29
  39.6 4.4 %fusion.54 = f32[32,8,1024]{2,0,1:T(8,128)S(1)} fusion(f32[8,1024,64]{2,1,0:T(8,128)S(1)} %bitcast.274, s32[]{:T(128)S(6)} %select_n.148, f32[32,64]{1,0:T(8,128)S(1)} %copy-done.29), kind=kOutput, calls=%fused_computation.163 | convolution fusion | flops 201328640 | bytes 3153924 | tf_op jit(solution)/shard_map/dot_general | solution.py:32
  44.0 4.9 %add_bitcast_fusion.4 = (f32[1,32,8,1024]{3,1,2,0:T(8,128)S(1)}, f32[1,32,8,1024]{3,1,2,0:T(8,128)S(1)}) fusion(f32[32,8,1024]{2,0,1:T(8,128)S(1)} %fusion.54, f32[32,1024]{1,0:T(8,128)S(1)} %copy-done.24, f32[32,1024]{1,0:T(8,128)S(1)} %copy-done.25, f32[8,1024,64]{2,1,0:T(8,128)S(1)} %bitcast.263, s32[]{:T(128)S(6)} %select_n.148, f32[32,64]{1,0:T(8,128)S(1)} %copy-done.29), kind=kOutput, calls=%fused_computation.75 | convolution fusion | flops 202901504 | bytes 5513220 | tf_op jit(solution)/shard_map/dot_general | solution.py:31
  49.2 1.8 collective-permute-start.1
  53.9 19.8 %collective-permute-done.1 = f32[2,32,8,512]{3,1,2,0:T(8,128)} collective-permute-done((f32[2,32,8,512]{3,1,2,0:T(8,128)S(1)}, f32[2,32,8,512]{3,1,2,0:T(8,128)}, u32[]{:S(2)}, u32[]{:S(2)}) %collective-permute-start.1) | collective-permute-done | bytes 1048608 | tf_op jit(solution)/shard_map/ppermute | solution.py:8
  73.7 2.1 slice_bitcast_fusion.14
  77.8 1.9 copy.23
  81.2 3.1 broadcast_in_dim.30
  85.2 4.4 %fusion.50 = f32[32,8,1024]{2,0,1:T(8,128)S(1)} fusion(f32[8,1024,64]{2,1,0:T(8,128)S(1)} %bitcast.276, s32[]{:T(128)S(6)} %select_n.146, f32[32,64]{1,0:T(8,128)S(1)} %copy-done.28), kind=kOutput, calls=%fused_computation.161 | convolution fusion | flops 201328640 | bytes 3153924 | tf_op jit(solution)/shard_map/dot_general | solution.py:32
  89.7 4.7 %add_bitcast_fusion.3 = (f32[1,32,8,1024]{3,1,2,0:T(8,128)S(1)}, f32[1,32,8,1024]{3,1,2,0:T(8,128)S(1)}) fusion(f32[32,8,1024]{2,0,1:T(8,128)S(1)} %fusion.50, f32[32,1024]{1,0:T(8,128)S(1)} %copy-done.22, f32[32,1024]{1,0:T(8,128)S(1)} %copy-done.23, f32[8,1024,64]{2,1,0:T(8,128)S(1)} %bitcast.264, s32[]{:T(128)S(6)} %select_n.146, f32[32,64]{1,0:T(8,128)S(1)} %copy-done.28), kind=kOutput, calls=%fused_computation.73 | convolution fusion | flops 202901504 | bytes 5513220 | tf_op jit(solution)/shard_map/dot_general | solution.py:31
  94.8 2.8 fusion.27
  100.5 2.1 slice_bitcast_fusion.10
  104.6 1.9 copy.31
  108.0 3.1 broadcast_in_dim.32
  112.0 4.4 %fusion.46 = f32[32,8,1024]{2,0,1:T(8,128)S(1)} fusion(f32[8,1024,64]{2,1,0:T(8,128)S(1)} %bitcast.278, s32[]{:T(128)S(6)} %select_n.144, f32[32,64]{1,0:T(8,128)S(1)} %copy-done.27), kind=kOutput, calls=%fused_computation.159 | convolution fusion | flops 201328640 | bytes 3153924 | tf_op jit(solution)/shard_map/dot_general | solution.py:32
  116.5 4.5 %add_bitcast_fusion.2 = (f32[1,32,8,1024]{3,1,2,0:T(8,128)S(1)}, f32[1,32,8,1024]{3,1,2,0:T(8,128)S(1)}) fusion(f32[32,8,1024]{2,0,1:T(8,128)S(1)} %fusion.46, f32[32,1024]{1,0:T(8,128)S(1)} %copy-done.20, f32[32,1024]{1,0:T(8,128)S(1)} %copy-done.21, f32[8,1024,64]{2,1,0:T(8,128)S(1)} %bitcast.265, s32[]{:T(128)S(6)} %select_n.144, f32[32,64]{1,0:T(8,128)S(1)} %copy-done.27), kind=kOutput, calls=%fused_computation.71 | convolution fusion | flops 202901504 | bytes 5513220 | tf_op jit(solution)/shard_map/dot_general | solution.py:31
  121.2 1.6 collective-permute-start.3
  126.1 20.7 %collective-permute-done.3 = f32[2,32,8,512]{3,1,2,0:T(8,128)} collective-permute-done((f32[2,32,8,512]{3,1,2,0:T(8,128)S(1)}, f32[2,32,8,512]{3,1,2,0:T(8,128)}, u32[]{:S(2)}, u32[]{:S(2)}) %collective-permute-start.3) | collective-permute-done | bytes 1048608 | tf_op jit(solution)/shard_map/ppermute | solution.py:8
  146.8 2.1 slice_bitcast_fusion.6
  150.9 1.9 copy.39
  154.3 3.1 broadcast_in_dim.34
  158.4 4.4 %fusion.42 = f32[32,8,1024]{2,0,1:T(8,128)S(1)} fusion(f32[8,1024,64]{2,1,0:T(8,128)S(1)} %bitcast.280, s32[]{:T(128)S(6)} %select_n.142, f32[32,64]{1,0:T(8,128)S(1)} %copy-done.26), kind=kOutput, calls=%fused_computation.157 | convolution fusion | flops 201328640 | bytes 3153924 | tf_op jit(solution)/shard_map/dot_general | solution.py:32
  162.8 4.5 %add_bitcast_fusion.1 = (f32[1,32,8,1024]{3,1,2,0:T(8,128)S(1)}, f32[1,32,8,1024]{3,1,2,0:T(8,128)S(1)}) fusion(f32[32,8,1024]{2,0,1:T(8,128)S(1)} %fusion.42, f32[32,1024]{1,0:T(8,128)S(1)} %copy-done.18, f32[32,1024]{1,0:T(8,128)S(1)} %copy-done.19, f32[8,1024,64]{2,1,0:T(8,128)S(1)} %bitcast.266, s32[]{:T(128)S(6)} %select_n.142, f32[32,64]{1,0:T(8,128)S(1)} %copy-done.26), kind=kOutput, calls=%fused_computation.69 | convolution fusion | flops 202901504 | bytes 5513220 | tf_op jit(solution)/shard_map/dot_general | solution.py:31
  167.6 2.6 collective-permute-start.4
  174.2 41.5 %collective-permute-done.4 = f32[2,32,8,512]{3,1,2,0:T(8,128)} collective-permute-done((f32[2,32,8,512]{3,1,2,0:T(8,128)S(1)}, f32[2,32,8,512]{3,1,2,0:T(8,128)}, u32[]{:S(2)}, u32[]{:S(2)}) %collective-permute-start.4) | collective-permute-done | bytes 1048608 | tf_op jit(solution)/shard_map/ppermute | solution.py:8
  215.7 2.1 slice_bitcast_fusion.2
  219.8 1.9 copy.47
  223.2 3.1 broadcast_in_dim.36
  227.2 4.4 %fusion.38 = f32[32,8,1024]{2,0,1:T(8,128)S(1)} fusion(f32[8,1024,64]{2,1,0:T(8,128)S(1)} %bitcast.272, s32[]{:T(128)S(6)} %select_n.140, f32[32,64]{1,0:T(8,128)S(1)} %get-tuple-element.80), kind=kOutput, calls=%fused_computation.155 | convolution fusion | flops 201328640 | bytes 3153924 | tf_op jit(solution)/shard_map/dot_general | solution.py:32
  231.7 4.5 %subtract_bitcast_fusion = (f32[1,32,8,1024]{3,1,2,0:T(8,128)S(1)}, f32[1,32,8,1024]{3,1,2,0:T(8,128)S(1)}) fusion(f32[32,8,1024]{2,0,1:T(8,128)S(1)} %fusion.38, f32[32,1024]{1,0:T(8,128)S(1)} %copy-done.17, f32[32,1024]{1,0:T(8,128)S(1)} %get-tuple-element.60, f32[8,1024,64]{2,1,0:T(8,128)S(1)} %bitcast.262, s32[]{:T(128)S(6)} %select_n.140, ...), kind=kOutput, calls=%fused_computation.68 | convolution fusion | flops 202901504 | bytes 5513220 | tf_op jit(solution)/shard_map/dot_general | solution.py:31
  236.4 5.0 %copy.55 = f32[2,32,8,1024]{1,2,3,0:T(8,128)} copy(f32[2,32,8,1024]{3,1,2,0:T(8,128)S(1)} %pad_maximum_fusion) | data formatting | bytes 4194304 | tf_op jit(solution)/shard_map/stack | solution.py:60
  241.4 13.0 %gather_fusion = f32[1024,2,32,8]{2,3,1,0:T(8,128)} fusion(f32[2,32,8,1024]{1,2,3,0:T(8,128)} %copy.55, s32[1024]{0:T(1024)S(1)} %broadcast_clamp_fusion), kind=kCustom, calls=%fused_computation | custom fusion | bytes 4198400 | tf_op jit(solution)/shard_map/jit(_take)/gather | solution.py:74
  254.3 8.6 %fusion.68 = f32[1024,2,8,32]{3,2,1,0:T(8,128)} fusion(f32[1024,2,32,8]{2,3,1,0:T(8,128)} %gather_fusion, pred[1024]{0:T(1024)(128)(4,1)S(1)} %compare_and_fusion), kind=kLoop, calls=%fused_computation.177 | loop fusion | flops 524288 | bytes 4195328
  263.0 6.8 %reshape.237 = f32[32,1,16384]{2,1,0:T(1,128)S(1)} reshape(f32[1024,2,8,32]{3,2,1,0:T(8,128)} %fusion.68) | data formatting | bytes 4194304
  269.8 55.6 %all_to_all.5 = f32[32,1,16384]{2,1,0:T(1,128)} all-to-all(f32[32,1,16384]{2,1,0:T(1,128)S(1)} %reshape.237), channel_id=1, replica_groups=mesh['lo'=4,'hi'=8] {'lo','hi'}, dimensions={0} | all-to-all | bytes 4194304 | tf_op jit(solution)/shard_map/all_to_all | solution.py:75
  325.9 7.4 %reduce = f32[32,16384]{1,0:T(8,128)S(1)} reduce(f32[32,1,16384]{2,1,0:T(1,128)} %all_to_all.5, f32[]{:T(128)} %broadcast.89), dimensions={1}, to_apply=%all_to_all.3.reduce_sub_computation | reduce | bytes 4194308 | tf_op jit(solution)/shard_map/all_to_all | solution.py:75
  333.3 4.8 %reshape.238 = f32[1024,2,8,32]{3,2,1,0:T(8,128)} reshape(f32[32,16384]{1,0:T(8,128)S(1)} %reduce) | data formatting | bytes 4194304
  338.2 6.6 %copy.56 = f32[2,32,8,1024]{3,2,1,0:T(8,128)} copy(f32[2,32,8,1024]{1,2,0,3:T(8,128)} %bitcast.261) | data formatting | bytes 4194304 | tf_op jit(solution)/shard_map/all_to_all | solution.py:75
  (114 shorter events, 37.2 us)
Async XLA Ops:
  0.0 14.0 %copy-start.10 = (f32[2,32,8,1024]{3,2,1,0:T(8,128)S(1)}, f32[2,32,8,1024]{3,2,1,0:T(8,128)}, u32[]{:S(2)}) copy-start(f32[2,32,8,1024]{3,2,1,0:T(8,128)} %param.9) | copy-start | bytes 6291460
  1.4 12.6 %copy-start.30 = (f32[5,32,64]{2,1,0:T(8,128)S(1)}, f32[5,32,64]{2,1,0:T(8,128)}, u32[]{:S(2)}) copy-start(f32[5,32,64]{2,1,0:T(8,128)} %param.12) | copy-start | bytes 122884
  1.5 26.3 %collective-permute-start = (f32[2,32,8,512]{3,2,1,0:T(8,128)S(1)}, f32[2,32,8,512]{3,2,1,0:T(8,128)}, u32[]{:S(2)}, u32[]{:S(2)}) collective-permute-start(f32[2,32,8,512]{3,2,1,0:T(8,128)S(1)} %constant_dynamic-slice_fusion), channel_id=1, source_target_pairs={{0,8},{8,0},{16,24},{24,16},{1,9},{9,1},{17,25},{25,17},{2,10},{10... | collective-permute-start | bytes 3145736 | tf_op jit(solution)/shard_map/ppermute | solution.py:8
  35.5 3.1 copy-start
  35.5 3.1 copy-start.1
  38.7 0.9 copy-start.29
  39.5 4.5 %copy-start.24 = (f32[32,1024]{1,0:T(8,128)S(1)}, f32[32,1024]{1,0:T(8,128)}, u32[]{:S(2)}) copy-start(f32[32,1024]{1,0:T(8,128)} %get-tuple-element.61) | copy-start | bytes 393220
  39.6 4.5 %copy-start.25 = (f32[32,1024]{1,0:T(8,128)S(1)}, f32[32,1024]{1,0:T(8,128)}, u32[]{:S(2)}) copy-start(f32[32,1024]{1,0:T(8,128)} %get-tuple-element.68) | copy-start | bytes 393220
  44.0 7.0 %copy-start.16 = (f32[64,1024]{1,0:T(8,128)S(1)}, f32[64,1024]{1,0:T(8,128)}, u32[]{:S(2)}) copy-start(f32[64,1024]{1,0:T(8,128)} %get-tuple-element.88) | copy-start | bytes 786436
  49.0 3.0 copy-start.15
  49.2 24.5 %collective-permute-start.1 = (f32[2,32,8,512]{3,1,2,0:T(8,128)S(1)}, f32[2,32,8,512]{3,1,2,0:T(8,128)}, u32[]{:S(2)}, u32[]{:S(2)}) collective-permute-start(f32[2,32,8,512]{3,1,2,0:T(8,128)S(1)} %get-tuple-element.34), channel_id=1, source_target_pairs={{0,16},{8,24},{16,0},{24,8},{1,17},{9,25},{17,1},{25,9},{2,18},{10... | collective-permute-start | bytes 3145736 | tf_op jit(solution)/shard_map/ppermute | solution.py:8
  81.1 3.1 copy-start.4
  81.2 3.1 copy-start.6
  84.3 0.9 copy-start.28
  85.2 4.5 %copy-start.22 = (f32[32,1024]{1,0:T(8,128)S(1)}, f32[32,1024]{1,0:T(8,128)}, u32[]{:S(2)}) copy-start(f32[32,1024]{1,0:T(8,128)} %get-tuple-element.62) | copy-start | bytes 393220
  85.2 4.5 %copy-start.23 = (f32[32,1024]{1,0:T(8,128)S(1)}, f32[32,1024]{1,0:T(8,128)}, u32[]{:S(2)}) copy-start(f32[32,1024]{1,0:T(8,128)} %get-tuple-element.67) | copy-start | bytes 393220
  89.7 5.1 %copy-start.11 = (f32[64,1024]{1,0:T(8,128)S(1)}, f32[64,1024]{1,0:T(8,128)}, u32[]{:S(2)}) copy-start(f32[64,1024]{1,0:T(8,128)} %get-tuple-element.38) | copy-start | bytes 786436
  89.7 5.1 %copy-start.12 = (f32[64,1024]{1,0:T(8,128)S(1)}, f32[64,1024]{1,0:T(8,128)}, u32[]{:S(2)}) copy-start(f32[64,1024]{1,0:T(8,128)} %get-tuple-element.41) | copy-start | bytes 786436
  94.6 5.9 %collective-permute-start.2 = (f32[2,32,8,512]{3,1,2,0:T(8,128)S(1)}, f32[2,32,8,512]{3,1,2,0:T(8,128)}, u32[]{:S(2)}, u32[]{:S(2)}) collective-permute-start(f32[2,32,8,512]{3,1,2,0:T(8,128)S(1)} %get-tuple-element.32), channel_id=1, source_target_pairs={{0,1},{1,0},{2,3},{3,2},{4,5},{5,4},{6,7},{7,6},{8,9},{9,8},{10,11... | collective-permute-start | bytes 3145736 | tf_op jit(solution)/shard_map/ppermute | solution.py:8
  107.9 3.1 copy-start.5
  107.9 3.1 copy-start.7
  111.1 0.9 copy-start.27
  112.0 4.5 %copy-start.20 = (f32[32,1024]{1,0:T(8,128)S(1)}, f32[32,1024]{1,0:T(8,128)}, u32[]{:S(2)}) copy-start(f32[32,1024]{1,0:T(8,128)} %get-tuple-element.63) | copy-start | bytes 393220
  112.0 4.5 %copy-start.21 = (f32[32,1024]{1,0:T(8,128)S(1)}, f32[32,1024]{1,0:T(8,128)}, u32[]{:S(2)}) copy-start(f32[32,1024]{1,0:T(8,128)} %get-tuple-element.66) | copy-start | bytes 393220
  116.5 6.3 %copy-start.14 = (f32[64,1024]{1,0:T(8,128)S(1)}, f32[64,1024]{1,0:T(8,128)}, u32[]{:S(2)}) copy-start(f32[64,1024]{1,0:T(8,128)} %get-tuple-element.90) | copy-start | bytes 786436
  121.0 3.2 copy-start.13
  121.2 25.6 %collective-permute-start.3 = (f32[2,32,8,512]{3,1,2,0:T(8,128)S(1)}, f32[2,32,8,512]{3,1,2,0:T(8,128)}, u32[]{:S(2)}, u32[]{:S(2)}) collective-permute-start(f32[2,32,8,512]{3,1,2,0:T(8,128)S(1)} %get-tuple-element.30), channel_id=1, source_target_pairs={{0,2},{1,3},{2,0},{3,1},{4,6},{5,7},{6,4},{7,5},{8,10},{9,11},{10,... | collective-permute-start | bytes 3145736 | tf_op jit(solution)/shard_map/ppermute | solution.py:8
  154.3 3.1 copy-start.2
  154.3 3.1 copy-start.3
  157.4 0.9 copy-start.26
  158.3 4.5 %copy-start.18 = (f32[32,1024]{1,0:T(8,128)S(1)}, f32[32,1024]{1,0:T(8,128)}, u32[]{:S(2)}) copy-start(f32[32,1024]{1,0:T(8,128)} %get-tuple-element.64) | copy-start | bytes 393220
  158.3 4.5 %copy-start.19 = (f32[32,1024]{1,0:T(8,128)S(1)}, f32[32,1024]{1,0:T(8,128)}, u32[]{:S(2)}) copy-start(f32[32,1024]{1,0:T(8,128)} %get-tuple-element.69) | copy-start | bytes 393220
  167.4 6.0 %copy-start.31 = (s32[1,1024]{1,0:T(1,128)S(1)}, s32[1,1024]{1,0:T(1,128)}, u32[]{:S(2)}) copy-start(s32[1,1024]{1,0:T(1,128)} %param.13) | copy-start | bytes 12292
  167.6 48.2 %collective-permute-start.4 = (f32[2,32,8,512]{3,1,2,0:T(8,128)S(1)}, f32[2,32,8,512]{3,1,2,0:T(8,128)}, u32[]{:S(2)}, u32[]{:S(2)}) collective-permute-start(f32[2,32,8,512]{3,1,2,0:T(8,128)S(1)} %get-tuple-element.28), channel_id=1, source_target_pairs={{0,4},{1,5},{2,6},{3,7},{4,0},{5,1},{6,2},{7,3},{8,12},{9,13},{10,... | collective-permute-start | bytes 3145736 | tf_op jit(solution)/shard_map/ppermute | solution.py:8
  223.2 3.1 copy-start.8
  223.2 3.1 copy-start.9
  227.2 4.5 %copy-start.17 = (f32[32,1024]{1,0:T(8,128)S(1)}, f32[32,1024]{1,0:T(8,128)}, u32[]{:S(2)}) copy-start(f32[32,1024]{1,0:T(8,128)} %get-tuple-element.65) | copy-start | bytes 393220
where the time goes:
time: 349 us; the launch traced here: 345 us
  local copies, waits for them, and re-layouts  108 us (31%)
  waiting for transfers between devices  90.7 us (26%)
  blocking collectives  55.6 us (16%)
  matrix products  45.4 us (13%)
  other arithmetic  35.3 us (10%)
  starting transfers between devices  9.09 us (3%)
    ppermute x5, waiting for transfers between devices, from_partner(): lax.ppermute(x, axis, [(i, i ^ 1 << distance) for i in range(lax.axis_siz...  90.7 us
    all_to_all x1, blocking collectives, shards(): lax.all_to_all(taken, ('lo', 'hi'), split_axis=3, concat_axis=3, tiled=True)  55.6 us
    dot_general x5, matrix products, apply_cols(): jnp.dot(matrix, yre, precision=lax.Precision.HIGHEST, preferred_element_t...  23.2 us
    broadcast_in_dim x10, local copies, waits for them, and re-layouts, widen(): jnp.broadcast_to(part[:, :, :, None], (rows, count, half, 2))  22.8 us
    dot_general x5, matrix products, apply_cols(): jnp.dot(matrix, yim, precision=lax.Precision.HIGHEST, preferred_element_t...  22.2 us
    squeeze x10, local copies, waits for them, and re-layouts, level(): real = jnp.concatenate([kept[0], got[0]], axis=0)  13.2 us
    gather x1, local copies, waits for them, and re-layouts, shards(): taken = jnp.take(state, destination[0], axis=3)  13 us
    unnamed x66, local copies, waits for them, and re-layouts  11.8 us
  transfers between devices with their start and end apart: 5, of which 4 were waited for; matrix products, arithmetic and copies ran while one was open for 9% of the time, Pallas kernels for 0%

commit v1 on v0

v1 whole, which is shorter than its diff:
```python
import functools

import jax
import jax.numpy as jnp
from jax import lax
from jax.experimental import pallas as pl
from jax.experimental.pallas import tpu as pltpu
from jax.sharding import PartitionSpec as P

MESH = pl.DeviceIdType.MESH
LANES = 128
VC = 2
TILE_BITS = 3


def slot_orders(levels, bits):
    lay = {q: ("k", q) for q in range(bits)}
    orders = []
    for l in range(levels):
        tile = bits - 1 - l % TILE_BITS
        lane = bits - 1 - l
        if l >= TILE_BITS:
            lay[tile], lay[lane] = lay[lane], lay[tile]
        assert lay[tile] == ("k", bits - 1 - l)
        lay[tile] = ("b", l)
        order = {}
        for q, (kind, n) in lay.items():
            order[q] = n + l + 1 if kind == "k" else l - n
        orders.append(order)
    return orders


def to_logical(index, order):
    out = jnp.zeros_like(index)
    for q, p in order.items():
        out = out | (((index >> q) & 1) << p)
    return out


def to_internal(index, order):
    out = jnp.zeros_like(index)
    for q, p in order.items():
        out = out | (((index >> p) & 1) << q)
    return out


def sincos(x):
    y = 0.5 * x
    z = y * y
    s = -1.0 / 39916800
    for c in (1.0 / 362880, -1.0 / 5040, 1.0 / 120, -1.0 / 6, 1.0):
        s = s * z + c
    s = s * y
    c = 1.0 / 479001600
    for k in (-1.0 / 3628800, 1.0 / 40320, -1.0 / 720, 1.0 / 24, -0.5, 1.0):
        c = c * z + k
    return 2.0 * s * c, 1.0 - 2.0 * s * s


def at_tile(l, value, a, b):
    where = l % TILE_BITS
    rest = [a, b]
    rest.insert(where, value)
    return tuple(rest)


def split2(x):
    hi = x.astype(jnp.bfloat16)
    lo = (x - hi.astype(jnp.float32)).astype(jnp.bfloat16)
    return hi, lo


def kernel(
    levels, lo_bits, n_lo, n_hi,
    x_ref, ain_ref, aout_ref, w_ref, dest_ref, out_ref,
    st_ref, got_ref, cos_ref, sin_ref, wk_ref, split_ref, pick_ref, t_ref, r_ref,
    send_sem, recv_sem, tsend_sem, trecv_sem,
):
    chunks = x_ref.shape[0]
    rank = x_ref.shape[-2]
    slots = dest_ref.shape[0]
    bits = slots.bit_length() - 1
    n = n_lo * n_hi
    piece = slots // n
    orders = slot_orders(levels, bits)
    my_lo = lax.axis_index("lo")
    my_hi = lax.axis_index("hi")
    me = my_lo * n_hi + my_hi

    barrier = pltpu.get_barrier_semaphore()

    def greet(i, carry):
        other = lax.rem(me + i, n)
        pl.semaphore_signal(
            barrier, inc=1, device_id=(other // n_hi, lax.rem(other, n_hi)), device_id_type=MESH
        )
        return carry

    lax.fori_loop(1, n, greet, 0)

    def place(l):
        if l < lo_bits:
            axis, own, stride = "lo", my_lo, 2**l
        else:
            axis, own, stride = "hi", my_hi, 2 ** (l - lo_bits)
        side = lax.rem(own // stride, 2)
        return axis, side, own + stride * (1 - 2 * side)

    def state(l, c):
        return x_ref.at[c] if l == 0 else st_ref.at[l - 1, c]

    def exchange(l, c):
        axis, side, partner = place(l)
        where = l % TILE_BITS
        index = (slice(None),) * (2 + where) + (1 - side,)
        device = (partner, my_hi) if axis == "lo" else (my_lo, partner)
        return pltpu.make_async_remote_copy(
            src_ref=state(l, c).at[index],
            dst_ref=got_ref.at[l, c],
            send_sem=send_sem.at[l, c],
            recv_sem=recv_sem.at[l, c],
            device_id=device,
            device_id_type=MESH,
        )

    def prepare(l):
        _, side, _ = place(l)
        w = w_ref[l]
        turned = jnp.concatenate([w[:, rank:], w[:, :rank]], axis=1)
        w = jnp.where(side == 0, w, turned)
        hi, lo = split2(w)
        wk_ref[l] = jnp.concatenate([hi, hi, lo], axis=1)
        rows = 3 * rank
        angle = jnp.concatenate([ain_ref[l], aout_ref[l]], axis=0)
        hi, lo = split2(angle)
        split_ref[0:rows] = hi
        split_ref[rows:2 * rows] = lo
        left = angle - hi.astype(jnp.float32) - lo.astype(jnp.float32)
        split_ref[2 * rows:3 * rows] = left.astype(jnp.bfloat16)

        def body(u, carry):
            wide = 2 * LANES
            index = lax.broadcasted_iota(jnp.int32, (1, wide), 1) + u * wide
            source = to_logical(index, orders[l])
            ids = lax.broadcasted_iota(jnp.int32, (slots, wide), 0)
            hot = jnp.where(ids == source, 1.0, 0.0).astype(jnp.bfloat16)
            got = jnp.dot(split_ref[...], hot, preferred_element_type=jnp.float32)
            got = got[0:rows] + got[rows:2 * rows] + got[2 * rows:3 * rows]
            sine, cosine = sincos(got)
            for half in range(2):
                cols = slice(half * LANES, (half + 1) * LANES)
                for part in range(3):
                    band = slice(part * rank, (part + 1) * rank)
                    sin_ref[l, u * 2 + half, part] = sine[band, cols]
                    cos_ref[l, u * 2 + half, part] = cosine[band, cols]
            return carry

        lax.fori_loop(0, slots // (2 * LANES), body, 0)

    def prepare_pick():
        want = to_internal(dest_ref[...], orders[levels - 1])

        def body(u, carry):
            ids = lax.broadcasted_iota(jnp.int32, (slots, LANES), 1) + u * LANES
            pick_ref[u] = jnp.where(ids == want, 1.0, 0.0).astype(jnp.bfloat16)
            return carry

        lax.fori_loop(0, slots // LANES, body, 0)

    def compute(l, c):
        _, side, _ = place(l)
        src = state(l, c)

        def body(u, carry):
            a, b = u // 2, lax.rem(u, 2)
            kept = at_tile(l, side, a, b)
            kre = [src[(v, 0) + kept] for v in range(VC)]
            kim = [src[(v, 1) + kept] for v in range(VC)]
            gre = [got_ref[l, c, v, 0, a, b] for v in range(VC)]
            gim = [got_ref[l, c, v, 1, a, b] for v in range(VC)]
            columns = []
            tiles = []
            for bit in range(2):
                t9, t8, t7 = at_tile(l, bit, a, b)
                tile = t9 * 4 + t8 * 2 + t7
                tiles.append(tile)
                ck, sk = cos_ref[l, tile, side], sin_ref[l, tile, side]
                cg, sg = cos_ref[l, tile, 1 - side], sin_ref[l, tile, 1 - side]
                for v in range(VC):
                    columns.append(jnp.concatenate(
                        [kre[v] * ck - kim[v] * sk, gre[v] * cg - gim[v] * sg], axis=0))
                    columns.append(jnp.concatenate(
                        [kre[v] * sk + kim[v] * ck, gre[v] * sg + gim[v] * cg], axis=0))
            hi, lo = split2(jnp.concatenate(columns, axis=1))
            stacked = jnp.concatenate([hi, lo, hi], axis=0)
            mapped = jnp.dot(wk_ref[l], stacked, preferred_element_type=jnp.float32)
            for bit in range(2):
                co, so = cos_ref[l, tiles[bit], 2], sin_ref[l, tiles[bit], 2]
                where = at_tile(l, bit, a, b)
                for v in range(VC):
                    at = (bit * VC + v) * 2 * LANES
                    mre = mapped[:, at:at + LANES]
                    mim = mapped[:, at + LANES:at + 2 * LANES]
                    st_ref[(l, c, v, 0) + where] = mre * co - mim * so
                    st_ref[(l, c, v, 1) + where] = mre * so + mim * co
            return carry

        lax.fori_loop(0, 4, body, 0)

    def swap(l, c):
        lane_bit = bits - 1 - l
        shift = 2**lane_bit
        lane = lax.broadcasted_iota(jnp.int32, (rank, LANES), 1)
        clear = ((lane >> lane_bit) & 1) == 0

        def body(u, carry):
            a, b = u // 2, lax.rem(u, 2)
            first, second = at_tile(l, 0, a, b), at_tile(l, 1, a, b)
            for v in range(VC):
                for part in range(2):
                    x = st_ref[(l - 1, c, v, part) + first]
                    y = st_ref[(l - 1, c, v, part) + second]
                    st_ref[(l - 1, c, v, part) + first] = jnp.where(clear, x, pltpu.roll(y, shift, 1))
                    st_ref[(l - 1, c, v, part) + second] = jnp.where(
                        clear, pltpu.roll(x, LANES - shift, 1), y)
            return carry

        lax.fori_loop(0, 4, body, 0)

    def relay(c, i):
        other = lax.rem(me + i, n)
        return pltpu.make_async_remote_copy(
            src_ref=t_ref.at[c, pl.ds(pl.multiple_of(other * piece, piece), piece)],
            dst_ref=r_ref.at[c, pl.ds(pl.multiple_of(me * piece, piece), piece)],
            send_sem=tsend_sem.at[c, i],
            recv_sem=trecv_sem.at[c, i],
            device_id=(other // n_hi, lax.rem(other, n_hi)),
            device_id_type=MESH,
        )

    def relay_in(c, i):
        other = lax.rem(me + n - i, n)
        return pltpu.make_async_remote_copy(
            src_ref=t_ref.at[c, pl.ds(pl.multiple_of(other * piece, piece), piece)],
            dst_ref=r_ref.at[c, pl.ds(pl.multiple_of(other * piece, piece), piece)],
            send_sem=tsend_sem.at[c, i],
            recv_sem=trecv_sem.at[c, i],
            device_id=(other // n_hi, lax.rem(other, n_hi)),
            device_id_type=MESH,
        )

    def gather(c):
        his, los = [], []
        total = None
        for tile in range(slots // LANES):
            where = (tile // 4, tile // 2 % 2, tile % 2)
            block = jnp.concatenate(
                [st_ref[(levels - 1, c, v, part) + where] for v in range(VC) for part in range(2)], axis=0)
            hi, lo = split2(block)
            his.append(jnp.concatenate([hi, lo], axis=0))
        both = jnp.concatenate(his, axis=1)
        split_at = both.shape[0] // 2

        def body(u, carry):
            rows = slots // 4
            at = pl.ds(pl.multiple_of(u * rows, rows), rows)
            hot = jnp.concatenate([pick_ref[t, at] for t in range(slots // LANES)], axis=1)
            got = lax.dot_general(
                hot, both, (((1,), (1,)), ((), ())), preferred_element_type=jnp.float32)
            t_ref[c, at] = got[:, :split_at] + got[:, split_at:]
            return carry

        lax.fori_loop(0, 4, body, 0)
        mine = pl.ds(pl.multiple_of(me * piece, piece), piece)
        r_ref[c, mine] = t_ref[c, mine]

        def send(i, carry):
            relay(c, i).start()
            return carry

        lax.fori_loop(1, n, send, 0)

    def finish(c):
        def wait(i, carry):
            relay_in(c, i).wait_recv()
            return carry

        lax.fori_loop(1, n, wait, 0)
        for g in range(slots // LANES):
            cols = slice(g * LANES, (g + 1) * LANES)
            out_ref[c, :, cols] = r_ref[c, cols].T

    pl.semaphore_wait(barrier, n - 1)
    for c in range(chunks):
        exchange(0, c).start()
    prepared = set()

    def need(l):
        if l < levels and l not in prepared:
            prepared.add(l)
            prepare(l)

    need(0)
    last = levels - 1
    order = sorted(
        ((c, l) for c in range(chunks) for l in range(levels)),
        key=lambda t: (t[0] + t[1] if t[1] < last else t[1] + 2 * t[0], -t[1]),
    )
    for c, l in order:
        need(l)
        exchange(l, c).wait_recv()
        compute(l, c)
        if l < last:
            if l + 1 >= TILE_BITS:
                swap(l + 1, c)
            exchange(l + 1, c).start()
            need(l + 1)
            if l + 1 == last and c == 0:
                prepare_pick()
        else:
            gather(c)
            if c > 0:
                finish(c - 1)
    finish(chunks - 1)
    for c in range(chunks):
        for l in range(levels):
            exchange(l, c).wait_send()

        def sent(i, carry):
            relay(c, i).wait_send()
            return carry

        lax.fori_loop(1, n, sent, 0)


def shards(coefficients, angle_in, angle_out, interp, destination):
    parts, rank, vectors, slots = coefficients.shape
    levels = interp.shape[0]
    n_lo, n_hi = lax.axis_size("lo"), lax.axis_size("hi")
    n = n_lo * n_hi
    chunks = vectors // VC
    x = coefficients.reshape(parts, rank, chunks, VC, 2, 2, 2, LANES)
    x = x.transpose(2, 3, 0, 4, 5, 6, 1, 7)
    rows = VC * parts * rank
    vmem = pl.BlockSpec(memory_space=pltpu.VMEM)
    f32, bf16 = jnp.float32, jnp.bfloat16
    tiles = slots // LANES
    out = pl.pallas_call(
        functools.partial(kernel, levels, n_lo.bit_length() - 1, n_lo, n_hi),
        out_shape=jax.ShapeDtypeStruct((chunks, rows, slots), f32),
        in_specs=[vmem] * 5,
        out_specs=vmem,
        scratch_shapes=[
            pltpu.VMEM((levels, chunks, VC, parts, 2, 2, 2, rank, LANES), f32),
            pltpu.VMEM((levels, chunks, VC, parts, 2, 2, rank, LANES), f32),
            pltpu.VMEM((levels, tiles, 3, rank, LANES), f32),
            pltpu.VMEM((levels, tiles, 3, rank, LANES), f32),
            pltpu.VMEM((levels, rank, 6 * rank), bf16),
            pltpu.VMEM((9 * rank, slots), bf16),
            pltpu.VMEM((tiles, slots, LANES), bf16),
            pltpu.VMEM((chunks, slots, rows), f32),
            pltpu.VMEM((chunks, slots, rows), f32),
            pltpu.SemaphoreType.DMA((levels, chunks)),
            pltpu.SemaphoreType.DMA((levels, chunks)),
            pltpu.SemaphoreType.DMA((chunks, n)),
            pltpu.SemaphoreType.DMA((chunks, n)),
        ],
        compiler_params=pltpu.CompilerParams(
            collective_id=0, has_side_effects=True, vmem_limit_bytes=56 * 1024 * 1024
        ),
    )(x, angle_in, angle_out, interp, destination.reshape(slots, 1))
    out = out.reshape(chunks, VC, parts, rank, slots).transpose(2, 3, 0, 1, 4)
    return out.reshape(parts, rank, vectors, slots)


def solution(mesh):
    placed = (
        P(None, None, None, ("lo", "hi")),
        P(None, None, ("lo", "hi")),
        P(None, None, ("lo", "hi")),
        P(),
        P(("lo", "hi"), None),
    )
    return jax.shard_map(
        shards,
        mesh=mesh,
        in_specs=placed,
        out_specs=P(None, None, None, ("lo", "hi")),
        check_vma=False,
    )
```

time: 349 us -> 147 us (0.42); the launches traced: 345 us -> 147 us
  Pallas kernels: 0 us -> 136 us
  local copies, waits for them, and re-layouts: 108 us -> 11.4 us
  waiting for transfers between devices: 90.7 us -> 0 us
  blocking collectives: 55.6 us -> 0 us
  matrix products: 45.4 us -> 0 us
  other arithmetic: 35.3 us -> 0 us
  starting transfers between devices: 9.09 us -> 0 us
    pallas_call x0 -> x1, Pallas kernels: none -> 136 us  [shards(): pl.pallas_call(functools.partial(kernel, levels, n_lo.bit_length() - 1, n...]
    ppermute x5 -> x0, waiting for transfers between devices: 90.7 us -> none  [from_partner(): lax.ppermute(x, axis, [(i, i ^ 1 << distance) for i in range(lax.axis_siz...]
    all_to_all x1 -> x0, blocking collectives: 55.6 us -> none  [shards(): lax.all_to_all(taken, ('lo', 'hi'), split_axis=3, concat_axis=3, tiled=True)]
    dot_general x10 -> x0, matrix products: 45.4 us -> none  [the longest x5 23.2 us: apply_cols(): jnp.dot(matrix, yre, precision=lax.Precision.HIGHEST, preferred_element_t...]
    broadcast_in_dim x10 -> x0, local copies, waits for them, and re-layouts: 22.8 us -> none  [widen(): jnp.broadcast_to(part[:, :, :, None], (rows, count, half, 2))]
    squeeze x12 -> x0, local copies, waits for them, and re-layouts: 16 us -> none  [the longest x10 13.2 us: level(): real = jnp.concatenate([kept[0], got[0]], axis=0)]
    concatenate x10 -> x0, local copies, waits for them, and re-layouts: 14 us -> none  [the longest x5 9.57 us: level(): real = jnp.concatenate([kept[0], got[0]], axis=0)]
    gather x1 -> x0, local copies, waits for them, and re-layouts: 13 us -> none  [shards(): taken = jnp.take(state, destination[0], axis=3)]
  transfers between devices with their start and end apart: 5 -> 0, of which waited for: 4 -> 0; matrix products, arithmetic and copies ran while one was open for 9% -> 0% of each run, Pallas kernels for 0% -> 0%
where the time goes in v1:
time: 147 us
  Pallas kernels  136 us (93%)
  local copies, waits for them, and re-layouts  11.4 us (8%)
    pallas_call x1, Pallas kernels, shards(): pl.pallas_call(functools.partial(kernel, levels, n_lo.bit_length() - 1, n...  136 us
    reshape x2, local copies, waits for them, and re-layouts, shards(): x = coefficients.reshape(parts, rank, chunks, VC, 2, 2, 2, LANES)  5.56 us
    reshape x1, local copies, waits for them, and re-layouts, shards(): return out.reshape(parts, rank, vectors, slots)  4.13 us

profile of v1, /device:TPU:0, one launch (start us, length us, event | category | flops | bytes accessed | tf_op | source)
XLA Modules:
  0.0 147.2 jit_solution(3059715976035581947)
XLA Ops:
  0.0 1.7 %copy.8.dest_ref = s32[1024,1]{1,0:T(8,128)} copy(s32[1024,1]{0,1:T(1,128)} %bitcast.13) | data formatting | bytes 8192 | tf_op jit(solution)/shard_map/reshape | solution.py:371
  1.7 3.0 %reshape.12 = f32[2,32,4,2,2,2,2,128]{7,6,5,4,3,2,1,0:T(2,128)S(1)} reshape(f32[2,32,8,1024]{3,2,1,0:T(8,128)} %param.5) | data formatting | bytes 4194304 | tf_op jit(solution)/shard_map/reshape | solution.py:342
  4.7 2.5 %copy.12 = f32[2,32,4,2,2,2,2,128]{7,1,6,5,4,0,3,2:T(8,128)} copy(f32[2,32,4,2,2,2,2,128]{7,6,5,4,3,2,1,0:T(2,128)S(1)} %reshape.12) | data formatting | bytes 4194304 | tf_op jit(solution)/shard_map/reshape | solution.py:342
  7.3 135.8 %shard_map.55 = f32[4,128,1024]{2,1,0:T(8,128)} custom-call(f32[4,2,2,2,2,2,32,128]{7,6,5,4,3,2,1,0:T(8,128)} %bitcast.11, f32[5,64,1024]{2,1,0:T(8,128)} %ain_ref.1, f32[5,32,1024]{2,1,0:T(8,128)} %aout_ref.1, f32[5,32,64]{2,1,0:T(8,128)} %w_ref.1, s32[1024,1]{1,0:T(8,128)} %copy.8.dest_ref), custom_call_target="tpu_custom_call" | custom-call | tf_op jit(solution)/shard_map/pallas_call | solution.py:348
  143.1 4.1 %copy.10 = f32[2,32,8,1024]{3,2,1,0:T(8,128)} copy(f32[2,32,8,1024]{3,1,0,2:T(8,128)} %bitcast.12) | data formatting | bytes 4194304 | tf_op jit(solution)/shard_map/reshape | solution.py:373

commit v2 on v1

--- a/solution.py
+++ b/solution.py
@@ -9,7 +9,8 @@
 
 MESH = pl.DeviceIdType.MESH
 LANES = 128
-VC = 2
+VC = 1
+PAIR = 2
 TILE_BITS = 3
 
 
@@ -73,12 +74,13 @@
 def kernel(
     levels, lo_bits, n_lo, n_hi,
     x_ref, ain_ref, aout_ref, w_ref, dest_ref, out_ref,
-    st_ref, got_ref, cos_ref, sin_ref, wk_ref, split_ref, pick_ref, t_ref, r_ref,
-    send_sem, recv_sem, tsend_sem, trecv_sem,
+    xs_ref, os_ref, first_ref, st_ref, got_ref, cos_ref, sin_ref, wk_ref, split_ref, pick_ref, t_ref, r_ref,
+    send_sem, recv_sem, tsend_sem, trecv_sem, x_sem, o_sem,
 ):
-    chunks = x_ref.shape[0]
-    rank = x_ref.shape[-2]
-    slots = dest_ref.shape[0]
+    chunks = st_ref.shape[1]
+    vectors = chunks * VC
+    rank = st_ref.shape[-2]
+    slots = dest_ref.shape[1]
     bits = slots.bit_length() - 1
     n = n_lo * n_hi
     piece = slots // n
@@ -89,6 +91,13 @@
 
     barrier = pltpu.get_barrier_semaphore()
 
+    def fetch(tile):
+        cols = pl.ds(tile * LANES, LANES)
+        return pltpu.make_async_copy(x_ref.at[:, cols], xs_ref.at[tile], x_sem.at[tile])
+
+    for tile in range(slots // LANES):
+        fetch(tile).start()
+
     def greet(i, carry):
         other = lax.rem(me + i, n)
         pl.semaphore_signal(
@@ -107,7 +116,7 @@
         return axis, side, own + stride * (1 - 2 * side)
 
     def state(l, c):
-        return x_ref.at[c] if l == 0 else st_ref.at[l - 1, c]
+        return first_ref.at[c] if l == 0 else st_ref.at[l - 1, c]
 
     def exchange(l, c):
         axis, side, partner = place(l)
@@ -135,37 +144,59 @@
         hi, lo = split2(angle)
         split_ref[0:rows] = hi
         split_ref[rows:2 * rows] = lo
-        left = angle - hi.astype(jnp.float32) - lo.astype(jnp.float32)
-        split_ref[2 * rows:3 * rows] = left.astype(jnp.bfloat16)
+        size = min(slots, 2 * LANES << l)
 
         def body(u, carry):
             wide = 2 * LANES
-            index = lax.broadcasted_iota(jnp.int32, (1, wide), 1) + u * wide
+            if l == 0:
+                tiles = (u, u + 4)
+                start = u * size
+            elif l == 1:
+                tiles = (u // 2 + lax.rem(u, 2) * 4, u // 2 + lax.rem(u, 2) * 4 + 2)
+                start = u // 2 * size
+            else:
+                tiles = (2 * u, 2 * u + 1)
+                start = 0
+            lane = lax.broadcasted_iota(jnp.int32, (1, wide), 1)
+            index = jnp.where(lane < LANES, lane + tiles[0] * LANES, lane + (tiles[1] - 1) * LANES)
             source = to_logical(index, orders[l])
-            ids = lax.broadcasted_iota(jnp.int32, (slots, wide), 0)
+            ids = lax.broadcasted_iota(jnp.int32, (size, wide), 0) + start
             hot = jnp.where(ids == source, 1.0, 0.0).astype(jnp.bfloat16)
-            got = jnp.dot(split_ref[...], hot, preferred_element_type=jnp.float32)
-            got = got[0:rows] + got[rows:2 * rows] + got[2 * rows:3 * rows]
+            if size == slots:
+                left = split_ref[...]
+            else:
+                left = split_ref[:, pl.ds(pl.multiple_of(start, size), size)]
+            got = jnp.dot(left, hot, preferred_element_type=jnp.float32)
+            got = got[0:rows] + got[rows:2 * rows]
             sine, cosine = sincos(got)
             for half in range(2):
                 cols = slice(half * LANES, (half + 1) * LANES)
                 for part in range(3):
                     band = slice(part * rank, (part + 1) * rank)
-                    sin_ref[l, u * 2 + half, part] = sine[band, cols]
-                    cos_ref[l, u * 2 + half, part] = cosine[band, cols]
+                    sin_ref[l, tiles[half], part] = sine[band, cols]
+                    cos_ref[l, tiles[half], part] = cosine[band, cols]
             return carry
 
         lax.fori_loop(0, slots // (2 * LANES), body, 0)
 
     def prepare_pick():
-        want = to_internal(dest_ref[...], orders[levels - 1])
-
-        def body(u, carry):
-            ids = lax.broadcasted_iota(jnp.int32, (slots, LANES), 1) + u * LANES
-            pick_ref[u] = jnp.where(ids == want, 1.0, 0.0).astype(jnp.bfloat16)
-            return carry
-
-        lax.fori_loop(0, slots // LANES, body, 0)
+        ids = lax.broadcasted_iota(jnp.int32, (LANES, LANES), 1).astype(jnp.float32)
+
+        for g in range(slots // LANES):
+            rows = slice(g * LANES, (g + 1) * LANES)
+            want = to_internal(dest_ref[:, rows], orders[levels - 1]).astype(jnp.float32)
+            want = jnp.broadcast_to(want, (LANES, LANES)).T
+
+            for u in range(slots // LANES):
+                hot = jnp.where(ids + float(u * LANES) == want, 1.0, 0.0)
+                pick_ref[u, rows] = hot.astype(jnp.bfloat16)
+
+    def load_first(c):
+        for v in range(VC):
+            for part in range(2):
+                rows = pl.ds(part * rank * vectors + c * VC + v, rank, stride=vectors)
+                for tile in range(slots // LANES):
+                    first_ref[c, v, part, tile // 4, tile // 2 % 2, tile % 2] = xs_ref[tile, rows, :]
 
     def compute(l, c):
         _, side, _ = place(l)
@@ -227,25 +258,35 @@
 
         lax.fori_loop(0, 4, body, 0)
 
+    def offsets(i):
+        step = i // n_lo
+        off_hi = n_hi // 2 + (step + 1) // 2 * (2 * lax.rem(step, 2) - 1)
+        return lax.rem(lax.rem(i, n_lo) + 1, n_lo), lax.rem(off_hi, n_hi)
+
     def relay(c, i):
-        other = lax.rem(me + i, n)
+        off_lo, off_hi = offsets(i)
+        to_lo, to_hi = lax.rem(my_lo + off_lo, n_lo), lax.rem(my_hi + off_hi, n_hi)
+        other = to_lo * n_hi + to_hi
         return pltpu.make_async_remote_copy(
             src_ref=t_ref.at[c, pl.ds(pl.multiple_of(other * piece, piece), piece)],
             dst_ref=r_ref.at[c, pl.ds(pl.multiple_of(me * piece, piece), piece)],
             send_sem=tsend_sem.at[c, i],
             recv_sem=trecv_sem.at[c, i],
-            device_id=(other // n_hi, lax.rem(other, n_hi)),
+            device_id=(to_lo, to_hi),
             device_id_type=MESH,
         )
 
     def relay_in(c, i):
-        other = lax.rem(me + n - i, n)
+        off_lo, off_hi = offsets(i)
+        to_lo = lax.rem(my_lo + n_lo - off_lo, n_lo)
+        to_hi = lax.rem(my_hi + n_hi - off_hi, n_hi)
+        other = to_lo * n_hi + to_hi
         return pltpu.make_async_remote_copy(
             src_ref=t_ref.at[c, pl.ds(pl.multiple_of(other * piece, piece), piece)],
             dst_ref=r_ref.at[c, pl.ds(pl.multiple_of(other * piece, piece), piece)],
             send_sem=tsend_sem.at[c, i],
             recv_sem=trecv_sem.at[c, i],
-            device_id=(other // n_hi, lax.rem(other, n_hi)),
+            device_id=(to_lo, to_hi),
             device_id_type=MESH,
         )
 
@@ -255,7 +296,7 @@
         for tile in range(slots // LANES):
             where = (tile // 4, tile // 2 % 2, tile % 2)
             block = jnp.concatenate(
-                [st_ref[(levels - 1, c, v, part) + where] for v in range(VC) for part in range(2)], axis=0)
+                [st_ref[(levels - 1, PAIR * c + v, 0, part) + where] for v in range(PAIR) for part in range(2)], axis=0)
             hi, lo = split2(block)
             his.append(jnp.concatenate([hi, lo], axis=0))
         both = jnp.concatenate(his, axis=1)
@@ -278,20 +319,36 @@
             relay(c, i).start()
             return carry
 
-        lax.fori_loop(1, n, send, 0)
+        lax.fori_loop(0, n - 1, send, 0)
+
+    def put(tile):
+        cols = pl.ds(tile * LANES, LANES)
+        return pltpu.make_async_copy(os_ref.at[tile], out_ref.at[:, cols], o_sem.at[tile])
 
     def finish(c):
         def wait(i, carry):
             relay_in(c, i).wait_recv()
             return carry
 
-        lax.fori_loop(1, n, wait, 0)
+        lax.fori_loop(0, n - 1, wait, 0)
         for g in range(slots // LANES):
             cols = slice(g * LANES, (g + 1) * LANES)
-            out_ref[c, :, cols] = r_ref[c, cols].T
-
+            block = r_ref[c, cols].T
+            for v in range(PAIR):
+                for part in range(2):
+                    at = (v * 2 + part) * rank
+                    rows = pl.ds(part * rank * vectors + c * PAIR + v, rank, stride=vectors)
+                    os_ref[g, rows, :] = block[at:at + rank]
+            if c == chunks // PAIR - 1:
+                put(g).start()
+
+    for tile in range(slots // LANES):
+        fetch(tile).wait()
+    load_first(0)
     pl.semaphore_wait(barrier, n - 1)
     for c in range(chunks):
+        if c > 0:
+            load_first(c)
         exchange(0, c).start()
     prepared = set()
 
@@ -304,7 +361,7 @@
     last = levels - 1
     order = sorted(
         ((c, l) for c in range(chunks) for l in range(levels)),
-        key=lambda t: (t[0] + t[1] if t[1] < last else t[1] + 2 * t[0], -t[1]),
+        key=lambda t: (t[0] + t[1] if t[1] < last else t[1] + 2 * t[0] + 1.5, -t[1]),
     )
     for c, l in order:
         need(l)
@@ -317,20 +374,23 @@
             need(l + 1)
             if l + 1 == last and c == 0:
                 prepare_pick()
-        else:
-            gather(c)
-            if c > 0:
-                finish(c - 1)
-    finish(chunks - 1)
+        elif c % PAIR == PAIR - 1:
+            gather(c // PAIR)
+            if c >= PAIR:
+                finish(c // PAIR - 1)
+    finish(chunks // PAIR - 1)
+    for tile in range(slots // LANES):
+        put(tile).wait()
     for c in range(chunks):
         for l in range(levels):
             exchange(l, c).wait_send()
+    for c in range(chunks // PAIR):
 
         def sent(i, carry):
             relay(c, i).wait_send()
             return carry
 
-        lax.fori_loop(1, n, sent, 0)
+        lax.fori_loop(0, n - 1, sent, 0)
 
 
 def shards(coefficients, angle_in, angle_out, interp, destination):
@@ -339,37 +399,40 @@
     n_lo, n_hi = lax.axis_size("lo"), lax.axis_size("hi")
     n = n_lo * n_hi
     chunks = vectors // VC
-    x = coefficients.reshape(parts, rank, chunks, VC, 2, 2, 2, LANES)
-    x = x.transpose(2, 3, 0, 4, 5, 6, 1, 7)
-    rows = VC * parts * rank
+    pairs = vectors // PAIR
+    rows = PAIR * parts * rank
     vmem = pl.BlockSpec(memory_space=pltpu.VMEM)
     f32, bf16 = jnp.float32, jnp.bfloat16
     tiles = slots // LANES
     out = pl.pallas_call(
         functools.partial(kernel, levels, n_lo.bit_length() - 1, n_lo, n_hi),
-        out_shape=jax.ShapeDtypeStruct((chunks, rows, slots), f32),
-        in_specs=[vmem] * 5,
-        out_specs=vmem,
+        out_shape=jax.ShapeDtypeStruct((parts * rank * vectors, slots), f32),
+        in_specs=[pl.BlockSpec(memory_space=pl.ANY)] + [vmem] * 4,
+        out_specs=pl.BlockSpec(memory_space=pl.ANY),
         scratch_shapes=[
+            pltpu.VMEM((tiles, parts * rank * vectors, LANES), f32),
+            pltpu.VMEM((tiles, parts * rank * vectors, LANES), f32),
+            pltpu.VMEM((chunks, VC, parts, 2, 2, 2, rank, LANES), f32),
             pltpu.VMEM((levels, chunks, VC, parts, 2, 2, 2, rank, LANES), f32),
             pltpu.VMEM((levels, chunks, VC, parts, 2, 2, rank, LANES), f32),
             pltpu.VMEM((levels, tiles, 3, rank, LANES), f32),
             pltpu.VMEM((levels, tiles, 3, rank, LANES), f32),
             pltpu.VMEM((levels, rank, 6 * rank), bf16),
-            pltpu.VMEM((9 * rank, slots), bf16),
+            pltpu.VMEM((6 * rank, slots), bf16),
             pltpu.VMEM((tiles, slots, LANES), bf16),
-            pltpu.VMEM((chunks, slots, rows), f32),
-            pltpu.VMEM((chunks, slots, rows), f32),
+            pltpu.VMEM((pairs, slots, rows), f32),
+            pltpu.VMEM((pairs, slots, rows), f32),
             pltpu.SemaphoreType.DMA((levels, chunks)),
             pltpu.SemaphoreType.DMA((levels, chunks)),
-            pltpu.SemaphoreType.DMA((chunks, n)),
-            pltpu.SemaphoreType.DMA((chunks, n)),
+            pltpu.SemaphoreType.DMA((pairs, n)),
+            pltpu.SemaphoreType.DMA((pairs, n)),
+            pltpu.SemaphoreType.DMA((tiles,)),
+            pltpu.SemaphoreType.DMA((tiles,)),
         ],
         compiler_params=pltpu.CompilerParams(
             collective_id=0, has_side_effects=True, vmem_limit_bytes=56 * 1024 * 1024
         ),
-    )(x, angle_in, angle_out, interp, destination.reshape(slots, 1))
-    out = out.reshape(chunks, VC, parts, rank, slots).transpose(2, 3, 0, 1, 4)
+    )(coefficients.reshape(-1, slots), angle_in, angle_out, interp, destination)
     return out.reshape(parts, rank, vectors, slots)
 
 

time: 147 us -> 134 us (0.912)
  local copies, waits for them, and re-layouts: 11.4 us -> 3.16 us
  Pallas kernels: 136 us -> 130 us
    reshape x4 -> x0, local copies, waits for them, and re-layouts: 11.4 us -> none  [the longest x2 5.56 us: shards(): x = coefficients.reshape(parts, rank, chunks, VC, 2, 2, 2, LANES)]
    pallas_call x1, Pallas kernels: 136 us -> 130 us  [shards(): pl.pallas_call(functools.partial(kernel, levels, n_lo.bit_length() - 1, n...]
    unnamed x0 -> x1, local copies, waits for them, and re-layouts: none -> 3.16 us
where the time goes in v2:
time: 134 us
  Pallas kernels  130 us (97%)
  local copies, waits for them, and re-layouts  3.16 us (2%)
    pallas_call x1, Pallas kernels, shards(): pl.pallas_call(functools.partial(kernel, levels, n_lo.bit_length() - 1, n...  130 us
    unnamed x1, local copies, waits for them, and re-layouts  3.16 us

profile of v2, /device:TPU:0, one launch (start us, length us, event | category | flops | bytes accessed | tf_op | source)
XLA Modules:
  0.0 133.6 jit_solution(14000160421086371431)
XLA Ops:
  0.0 130.4 %shard_map.55 = f32[512,1024]{1,0:T(8,128)} custom-call(f32[512,1024]{1,0:T(8,128)} %bitcast.3, f32[5,64,1024]{2,1,0:T(8,128)} %ain_ref.1, f32[5,32,1024]{2,1,0:T(8,128)} %aout_ref.1, f32[5,32,64]{2,1,0:T(8,128)} %w_ref.1, s32[1,1024]{1,0:T(1,128)} %dest_ref.1), custom_call_target="tpu_custom_call" | custom-call | tf_op jit(solution)/shard_map/pallas_call | solution.py:407
  130.4 3.2 %copy.7 = f32[2,32,8,1024]{3,2,1,0:T(8,128)} copy(f32[2,32,8,1024]{3,2,1,0:T(8,128)} %bitcast.2) | data formatting | bytes 4194304

commit v3 on v2

--- a/solution.py
+++ b/solution.py
@@ -11,6 +11,7 @@
 LANES = 128
 VC = 1
 PAIR = 2
+AHEAD = 4
 TILE_BITS = 3
 
 
@@ -73,9 +74,9 @@
 
 def kernel(
     levels, lo_bits, n_lo, n_hi,
-    x_ref, ain_ref, aout_ref, w_ref, dest_ref, out_ref,
-    xs_ref, os_ref, first_ref, st_ref, got_ref, cos_ref, sin_ref, wk_ref, split_ref, pick_ref, t_ref, r_ref,
-    send_sem, recv_sem, tsend_sem, trecv_sem, x_sem, o_sem,
+    x_ref, ain_hbm, aout_hbm, w_ref, dest_ref, out_ref,
+    ain_ref, aout_ref, xs_ref, os_ref, first_ref, st_ref, got_ref, cos_ref, sin_ref, wk_ref, split_ref, pick_ref, t_ref, r_ref,
+    send_sem, recv_sem, tsend_sem, trecv_sem, x_sem, o_sem, a_sem,
 ):
     chunks = st_ref.shape[1]
     vectors = chunks * VC
@@ -97,6 +98,16 @@
 
     for tile in range(slots // LANES):
         fetch(tile).start()
+
+    def fetch_angles(l):
+        return (
+            pltpu.make_async_copy(ain_hbm.at[l], ain_ref.at[l], a_sem.at[0, l]),
+            pltpu.make_async_copy(aout_hbm.at[l], aout_ref.at[l], a_sem.at[1, l]),
+        )
+
+    for l in range(levels):
+        for copy in fetch_angles(l):
+            copy.start()
 
     def greet(i, carry):
         other = lax.rem(me + i, n)
@@ -140,6 +151,8 @@
         hi, lo = split2(w)
         wk_ref[l] = jnp.concatenate([hi, hi, lo], axis=1)
         rows = 3 * rank
+        for copy in fetch_angles(l):
+            copy.wait()
         angle = jnp.concatenate([ain_ref[l], aout_ref[l]], axis=0)
         hi, lo = split2(angle)
         split_ref[0:rows] = hi
@@ -236,7 +249,7 @@
                     st_ref[(l, c, v, 1) + where] = mre * so + mim * co
             return carry
 
-        lax.fori_loop(0, 4, body, 0)
+        lax.fori_loop(0, 4, body, 0, unroll=2)
 
     def swap(l, c):
         lane_bit = bits - 1 - l
@@ -346,9 +359,9 @@
         fetch(tile).wait()
     load_first(0)
     pl.semaphore_wait(barrier, n - 1)
-    for c in range(chunks):
-        if c > 0:
-            load_first(c)
+    exchange(0, 0).start()
+    for c in range(1, AHEAD):
+        load_first(c)
         exchange(0, c).start()
     prepared = set()
 
@@ -367,6 +380,9 @@
         need(l)
         exchange(l, c).wait_recv()
         compute(l, c)
+        if l == 0 and c + AHEAD < chunks:
+            load_first(c + AHEAD)
+            exchange(0, c + AHEAD).start()
         if l < last:
             if l + 1 >= TILE_BITS:
                 swap(l + 1, c)
@@ -376,9 +392,8 @@
                 prepare_pick()
         elif c % PAIR == PAIR - 1:
             gather(c // PAIR)
-            if c >= PAIR:
-                finish(c // PAIR - 1)
-    finish(chunks // PAIR - 1)
+    for c in range(chunks // PAIR):
+        finish(c)
     for tile in range(slots // LANES):
         put(tile).wait()
     for c in range(chunks):
@@ -407,9 +422,11 @@
     out = pl.pallas_call(
         functools.partial(kernel, levels, n_lo.bit_length() - 1, n_lo, n_hi),
         out_shape=jax.ShapeDtypeStruct((parts * rank * vectors, slots), f32),
-        in_specs=[pl.BlockSpec(memory_space=pl.ANY)] + [vmem] * 4,
+        in_specs=[pl.BlockSpec(memory_space=pl.ANY)] * 3 + [vmem] * 2,
         out_specs=pl.BlockSpec(memory_space=pl.ANY),
         scratch_shapes=[
+            pltpu.VMEM((levels, 2 * rank, slots), f32),
+            pltpu.VMEM((levels, rank, slots), f32),
             pltpu.VMEM((tiles, parts * rank * vectors, LANES), f32),
             pltpu.VMEM((tiles, parts * rank * vectors, LANES), f32),
             pltpu.VMEM((chunks, VC, parts, 2, 2, 2, rank, LANES), f32),
@@ -428,6 +445,7 @@
             pltpu.SemaphoreType.DMA((pairs, n)),
             pltpu.SemaphoreType.DMA((tiles,)),
             pltpu.SemaphoreType.DMA((tiles,)),
+            pltpu.SemaphoreType.DMA((2, levels)),
         ],
         compiler_params=pltpu.CompilerParams(
             collective_id=0, has_side_effects=True, vmem_limit_bytes=56 * 1024 * 1024

time: 134 us -> 133 us (level)
  no operation moved by 1% of the time
where the time goes in v3:
time: 133 us
  Pallas kernels  130 us (98%)
  local copies, waits for them, and re-layouts  3.16 us (2%)
    pallas_call x1, Pallas kernels, shards(): pl.pallas_call(functools.partial(kernel, levels, n_lo.bit_length() - 1, n...  130 us
    unnamed x1, local copies, waits for them, and re-layouts  3.16 us

profile of v3, /device:TPU:0, one launch (start us, length us, event | category | flops | bytes accessed | tf_op | source)
XLA Modules:
  0.0 132.8 jit_solution(13610766102031199979)
XLA Ops:
  0.0 129.6 %shard_map.55 = f32[512,1024]{1,0:T(8,128)} custom-call(f32[512,1024]{1,0:T(8,128)} %bitcast.3, f32[5,64,1024]{2,1,0:T(8,128)} %ain_hbm.1, f32[5,32,1024]{2,1,0:T(8,128)} %aout_hbm.1, f32[5,32,64]{2,1,0:T(8,128)} %w_ref.1, s32[1,1024]{1,0:T(1,128)} %dest_ref.1), custom_call_target="tpu_custom_call" | custom-call | tf_op jit(solution)/shard_map/pallas_call | solution.py:422
  129.6 3.2 %copy.7 = f32[2,32,8,1024]{3,2,1,0:T(8,128)} copy(f32[2,32,8,1024]{3,2,1,0:T(8,128)} %bitcast.2) | data formatting | bytes 4194304

commit v4 on v3

--- a/solution.py
+++ b/solution.py
@@ -75,8 +75,8 @@
 def kernel(
     levels, lo_bits, n_lo, n_hi,
     x_ref, ain_hbm, aout_hbm, w_ref, dest_ref, out_ref,
-    ain_ref, aout_ref, xs_ref, os_ref, first_ref, st_ref, got_ref, cos_ref, sin_ref, wk_ref, split_ref, pick_ref, t_ref, r_ref,
-    send_sem, recv_sem, tsend_sem, trecv_sem, x_sem, o_sem, a_sem,
+    ain_ref, aout_ref, xs_ref, os_ref, first_ref, st_ref, got_ref, cos_ref, sin_ref, wk_ref, split_ref, pick_ref, t_ref, r_ref, b_ref,
+    send_sem, recv_sem, tsend_sem, trecv_sem, bsend_sem, brecv_sem, x_sem, o_sem, a_sem,
 ):
     chunks = st_ref.shape[1]
     vectors = chunks * VC
@@ -271,34 +271,59 @@
 
         lax.fori_loop(0, 4, body, 0)
 
+    half = n_hi // 2
+    mine_half = my_hi // half
+    within = lax.rem(my_hi, half)
+    opposite = lax.rem(my_hi + half, n_hi)
+
+    def rows_of(owner):
+        return pl.ds(pl.multiple_of(owner * piece, piece), piece)
+
+    def bulk(c, k):
+        to_lo = lax.rem(my_lo + k + 1, n_lo)
+        start = (to_lo * n_hi + (1 - mine_half) * half) * piece
+        size = half * piece
+        return pltpu.make_async_remote_copy(
+            src_ref=t_ref.at[c, pl.ds(pl.multiple_of(start, size), size)],
+            dst_ref=b_ref.at[c, to_lo],
+            send_sem=bsend_sem.at[c, k],
+            recv_sem=brecv_sem.at[c, k],
+            device_id=(my_lo, opposite),
+            device_id_type=MESH,
+        )
+
     def offsets(i):
-        step = i // n_lo
-        off_hi = n_hi // 2 + (step + 1) // 2 * (2 * lax.rem(step, 2) - 1)
-        return lax.rem(lax.rem(i, n_lo) + 1, n_lo), lax.rem(off_hi, n_hi)
-
-    def relay(c, i):
+        return lax.rem(i // half + 1, n_lo), lax.rem(lax.rem(i, half) + 1, half)
+
+    def relay(c, kind, i):
         off_lo, off_hi = offsets(i)
-        to_lo, to_hi = lax.rem(my_lo + off_lo, n_lo), lax.rem(my_hi + off_hi, n_hi)
-        other = to_lo * n_hi + to_hi
+        to_lo, to_in = lax.rem(my_lo + off_lo, n_lo), lax.rem(within + off_hi, half)
+        to_hi = mine_half * half + to_in
+        if kind == 0:
+            src = t_ref.at[c, rows_of(to_lo * n_hi + to_hi)]
+            dst = r_ref.at[c, rows_of(me)]
+        else:
+            src = b_ref.at[c, to_lo, rows_of(to_in)]
+            dst = r_ref.at[c, rows_of(my_lo * n_hi + opposite)]
         return pltpu.make_async_remote_copy(
-            src_ref=t_ref.at[c, pl.ds(pl.multiple_of(other * piece, piece), piece)],
-            dst_ref=r_ref.at[c, pl.ds(pl.multiple_of(me * piece, piece), piece)],
-            send_sem=tsend_sem.at[c, i],
-            recv_sem=trecv_sem.at[c, i],
+            src_ref=src,
+            dst_ref=dst,
+            send_sem=tsend_sem.at[c, kind, i],
+            recv_sem=trecv_sem.at[c, kind, i],
             device_id=(to_lo, to_hi),
             device_id_type=MESH,
         )
 
-    def relay_in(c, i):
+    def relay_in(c, kind, i):
         off_lo, off_hi = offsets(i)
         to_lo = lax.rem(my_lo + n_lo - off_lo, n_lo)
-        to_hi = lax.rem(my_hi + n_hi - off_hi, n_hi)
-        other = to_lo * n_hi + to_hi
+        to_hi = mine_half * half + lax.rem(within + half - off_hi, half)
+        source = to_lo * n_hi + (to_hi if kind == 0 else lax.rem(to_hi + half, n_hi))
         return pltpu.make_async_remote_copy(
-            src_ref=t_ref.at[c, pl.ds(pl.multiple_of(other * piece, piece), piece)],
-            dst_ref=r_ref.at[c, pl.ds(pl.multiple_of(other * piece, piece), piece)],
-            send_sem=tsend_sem.at[c, i],
-            recv_sem=trecv_sem.at[c, i],
+            src_ref=t_ref.at[c, rows_of(source)],
+            dst_ref=r_ref.at[c, rows_of(source)],
+            send_sem=tsend_sem.at[c, kind, i],
+            recv_sem=trecv_sem.at[c, kind, i],
             device_id=(to_lo, to_hi),
             device_id_type=MESH,
         )
@@ -325,14 +350,25 @@
             return carry
 
         lax.fori_loop(0, 4, body, 0)
-        mine = pl.ds(pl.multiple_of(me * piece, piece), piece)
-        r_ref[c, mine] = t_ref[c, mine]
+        for k in range(n_lo):
+            bulk(c, k).start()
+        r_ref[c, rows_of(me)] = t_ref[c, rows_of(me)]
 
         def send(i, carry):
-            relay(c, i).start()
-            return carry
-
-        lax.fori_loop(0, n - 1, send, 0)
+            relay(c, 0, i).start()
+            return carry
+
+        lax.fori_loop(0, n // 2 - 1, send, 0)
+
+    def forward(c):
+        def send(i, carry):
+            relay(c, 1, i).start()
+            return carry
+
+        for k in range(n_lo):
+            bulk(c, k).wait_recv()
+            lax.fori_loop(k * half, min((k + 1) * half, n // 2 - 1), send, 0)
+        r_ref[c, rows_of(my_lo * n_hi + opposite)] = b_ref[c, my_lo, rows_of(within)]
 
     def put(tile):
         cols = pl.ds(tile * LANES, LANES)
@@ -340,10 +376,11 @@
 
     def finish(c):
         def wait(i, carry):
-            relay_in(c, i).wait_recv()
-            return carry
-
-        lax.fori_loop(0, n - 1, wait, 0)
+            relay_in(c, 0, i).wait_recv()
+            relay_in(c, 1, i).wait_recv()
+            return carry
+
+        lax.fori_loop(0, n // 2 - 1, wait, 0)
         for g in range(slots // LANES):
             cols = slice(g * LANES, (g + 1) * LANES)
             block = r_ref[c, cols].T
@@ -392,6 +429,10 @@
                 prepare_pick()
         elif c % PAIR == PAIR - 1:
             gather(c // PAIR)
+            if c // PAIR >= 2:
+                forward(c // PAIR - 2)
+    for c in range(max(0, chunks // PAIR - 2), chunks // PAIR):
+        forward(c)
     for c in range(chunks // PAIR):
         finish(c)
     for tile in range(slots // LANES):
@@ -402,10 +443,13 @@
     for c in range(chunks // PAIR):
 
         def sent(i, carry):
-            relay(c, i).wait_send()
-            return carry
-
-        lax.fori_loop(0, n - 1, sent, 0)
+            relay(c, 0, i).wait_send()
+            relay(c, 1, i).wait_send()
+            return carry
+
+        lax.fori_loop(0, n // 2 - 1, sent, 0)
+        for k in range(n_lo):
+            bulk(c, k).wait_send()
 
 
 def shards(coefficients, angle_in, angle_out, interp, destination):
@@ -439,10 +483,13 @@
             pltpu.VMEM((tiles, slots, LANES), bf16),
             pltpu.VMEM((pairs, slots, rows), f32),
             pltpu.VMEM((pairs, slots, rows), f32),
+            pltpu.VMEM((pairs, n_lo, slots // n_lo // 2, rows), f32),
             pltpu.SemaphoreType.DMA((levels, chunks)),
             pltpu.SemaphoreType.DMA((levels, chunks)),
-            pltpu.SemaphoreType.DMA((pairs, n)),
-            pltpu.SemaphoreType.DMA((pairs, n)),
+            pltpu.SemaphoreType.DMA((pairs, 2, n // 2)),
+            pltpu.SemaphoreType.DMA((pairs, 2, n // 2)),
+            pltpu.SemaphoreType.DMA((pairs, n_lo)),
+            pltpu.SemaphoreType.DMA((pairs, n_lo)),
             pltpu.SemaphoreType.DMA((tiles,)),
             pltpu.SemaphoreType.DMA((tiles,)),
             pltpu.SemaphoreType.DMA((2, levels)),

time: 133 us -> 141 us (1.060)
  the two profiles are of different devices: /device:TPU:0 before, /device:TPU:17 now
where the time goes in v4:
time: 141 us; the launch traced here: 140 us
  Pallas kernels  137 us (97%)
  local copies, waits for them, and re-layouts  3.16 us (2%)
    pallas_call x1, Pallas kernels, shards(): pl.pallas_call(functools.partial(kernel, levels, n_lo.bit_length() - 1, n...  137 us
    unnamed x1, local copies, waits for them, and re-layouts  3.16 us

profile of v4, /device:TPU:17, one launch (start us, length us, event | category | flops | bytes accessed | tf_op | source)
XLA Modules:
  0.0 140.3 jit_solution(10616468355443712175)
XLA Ops:
  0.0 137.1 %shard_map.55 = f32[512,1024]{1,0:T(8,128)} custom-call(f32[512,1024]{1,0:T(8,128)} %bitcast.3, f32[5,64,1024]{2,1,0:T(8,128)} %ain_hbm.1, f32[5,32,1024]{2,1,0:T(8,128)} %aout_hbm.1, f32[5,32,64]{2,1,0:T(8,128)} %w_ref.1, s32[1,1024]{1,0:T(1,128)} %dest_ref.1), custom_call_target="tpu_custom_call" | custom-call | tf_op jit(solution)/shard_map/pallas_call | solution.py:466
  137.2 3.2 %copy.7 = f32[2,32,8,1024]{3,2,1,0:T(8,128)} copy(f32[2,32,8,1024]{3,2,1,0:T(8,128)} %bitcast.2) | data formatting | bytes 4194304

commit v5 on v3

--- a/solution.py
+++ b/solution.py
@@ -272,9 +272,10 @@
         lax.fori_loop(0, 4, body, 0)
 
     def offsets(i):
-        step = i // n_lo
-        off_hi = n_hi // 2 + (step + 1) // 2 * (2 * lax.rem(step, 2) - 1)
-        return lax.rem(lax.rem(i, n_lo) + 1, n_lo), lax.rem(off_hi, n_hi)
+        half = n_hi // 2
+        pair = i // 2
+        off_hi = half - 1 - pair // n_lo + half * (1 - lax.rem(i, 2))
+        return lax.rem(lax.rem(pair, n_lo) + 1, n_lo), lax.rem(off_hi, n_hi)
 
     def relay(c, i):
         off_lo, off_hi = offsets(i)
@@ -371,6 +372,7 @@
             prepare(l)
 
     need(0)
+    need(1)
     last = levels - 1
     order = sorted(
         ((c, l) for c in range(chunks) for l in range(levels)),
@@ -387,7 +389,10 @@
             if l + 1 >= TILE_BITS:
                 swap(l + 1, c)
             exchange(l + 1, c).start()
-            need(l + 1)
+            if l == 0:
+                need(2)
+            elif l >= 2:
+                need(l + 1)
             if l + 1 == last and c == 0:
                 prepare_pick()
         elif c % PAIR == PAIR - 1:

time: 133 us -> 139 us (1.045)
  Pallas kernels: 130 us -> 135 us
    pallas_call x1, Pallas kernels: 130 us -> 135 us  [shards(): pl.pallas_call(functools.partial(kernel, levels, n_lo.bit_length() - 1, n...]
where the time goes in v5:
time: 139 us; the launch traced here: 138 us
  Pallas kernels  135 us (97%)
  local copies, waits for them, and re-layouts  3.16 us (2%)
    pallas_call x1, Pallas kernels, shards(): pl.pallas_call(functools.partial(kernel, levels, n_lo.bit_length() - 1, n...  135 us
    unnamed x1, local copies, waits for them, and re-layouts  3.16 us

profile of v5, /device:TPU:0, one launch (start us, length us, event | category | flops | bytes accessed | tf_op | source)
XLA Modules:
  0.0 138.5 jit_solution(4460718736074761298)
XLA Ops:
  0.0 135.3 %shard_map.55 = f32[512,1024]{1,0:T(8,128)} custom-call(f32[512,1024]{1,0:T(8,128)} %bitcast.3, f32[5,64,1024]{2,1,0:T(8,128)} %ain_hbm.1, f32[5,32,1024]{2,1,0:T(8,128)} %aout_hbm.1, f32[5,32,64]{2,1,0:T(8,128)} %w_ref.1, s32[1,1024]{1,0:T(1,128)} %dest_ref.1), custom_call_target="tpu_custom_call" | custom-call | tf_op jit(solution)/shard_map/pallas_call | solution.py:427
  135.3 3.2 %copy.7 = f32[2,32,8,1024]{3,2,1,0:T(8,128)} copy(f32[2,32,8,1024]{3,2,1,0:T(8,128)} %bitcast.2) | data formatting | bytes 4194304

commit v6 on v3

--- a/solution.py
+++ b/solution.py
@@ -271,14 +271,20 @@
 
         lax.fori_loop(0, 4, body, 0)
 
-    def offsets(i):
-        step = i // n_lo
-        off_hi = n_hi // 2 + (step + 1) // 2 * (2 * lax.rem(step, 2) - 1)
-        return lax.rem(lax.rem(i, n_lo) + 1, n_lo), lax.rem(off_hi, n_hi)
+    half = n_hi // 2
+
+    def peer(i, sign):
+        own = i // (n // 2)
+        r = lax.rem(i, n // 2)
+        off_lo = lax.rem(lax.rem(r, n_lo) + 1, n_lo)
+        off_in = lax.rem(r // n_lo + 1, half)
+        to_lo = lax.rem(my_lo + n_lo + sign * off_lo, n_lo)
+        to_in = lax.rem(lax.rem(my_hi, half) + half + sign * off_in, half)
+        side = lax.rem(my_hi // half + 1 + own, 2)
+        return to_lo, side * half + to_in
 
     def relay(c, i):
-        off_lo, off_hi = offsets(i)
-        to_lo, to_hi = lax.rem(my_lo + off_lo, n_lo), lax.rem(my_hi + off_hi, n_hi)
+        to_lo, to_hi = peer(i, 1)
         other = to_lo * n_hi + to_hi
         return pltpu.make_async_remote_copy(
             src_ref=t_ref.at[c, pl.ds(pl.multiple_of(other * piece, piece), piece)],
@@ -290,9 +296,7 @@
         )
 
     def relay_in(c, i):
-        off_lo, off_hi = offsets(i)
-        to_lo = lax.rem(my_lo + n_lo - off_lo, n_lo)
-        to_hi = lax.rem(my_hi + n_hi - off_hi, n_hi)
+        to_lo, to_hi = peer(i, -1)
         other = to_lo * n_hi + to_hi
         return pltpu.make_async_remote_copy(
             src_ref=t_ref.at[c, pl.ds(pl.multiple_of(other * piece, piece), piece)],

time: 133 us -> 136 us (1.023)
  Pallas kernels: 130 us -> 133 us
    pallas_call x1, Pallas kernels: 130 us -> 133 us  [shards(): pl.pallas_call(functools.partial(kernel, levels, n_lo.bit_length() - 1, n...]
where the time goes in v6:
time: 136 us
  Pallas kernels  133 us (98%)
  local copies, waits for them, and re-layouts  3.16 us (2%)
    pallas_call x1, Pallas kernels, shards(): pl.pallas_call(functools.partial(kernel, levels, n_lo.bit_length() - 1, n...  133 us
    unnamed x1, local copies, waits for them, and re-layouts  3.16 us

profile of v6, /device:TPU:0, one launch (start us, length us, event | category | flops | bytes accessed | tf_op | source)
XLA Modules:
  0.0 135.8 jit_solution(11892091793842987376)
XLA Ops:
  0.0 132.6 %shard_map.55 = f32[512,1024]{1,0:T(8,128)} custom-call(f32[512,1024]{1,0:T(8,128)} %bitcast.3, f32[5,64,1024]{2,1,0:T(8,128)} %ain_hbm.1, f32[5,32,1024]{2,1,0:T(8,128)} %aout_hbm.1, f32[5,32,64]{2,1,0:T(8,128)} %w_ref.1, s32[1,1024]{1,0:T(1,128)} %dest_ref.1), custom_call_target="tpu_custom_call" | custom-call | tf_op jit(solution)/shard_map/pallas_call | solution.py:426
  132.6 3.2 %copy.7 = f32[2,32,8,1024]{3,2,1,0:T(8,128)} copy(f32[2,32,8,1024]{3,2,1,0:T(8,128)} %bitcast.2) | data formatting | bytes 4194304
